TPU v7x, 32 devices: a whole 2x2x4 slice. The times are simulated.
32 devices in a mesh: section: 2 (over y), dp: 2 (over x), ctx: 8 (over z, core).
Axes of the slice: x: 2, y: 2, z: 4, core: 2. Of those that a mesh axis runs over, the one named last changes fastest.
Arguments:
- inputs: bfloat16 [2, 2, 1024, 1024], P(None, 'dp', 'ctx'), may hold values from -6 to 6
- segments: int32 [2, 2, 1024], P(None, 'dp'), may hold values from 0 to 17, as said below
- cotangent: bfloat16 [2, 2, 1024, 1024], P(None, 'dp', 'ctx'), may hold values from -6 to 6
- norm_gain: bfloat16 [2, 1024], P('section', ('dp', 'ctx')), may hold values from 0.5 to 1.5
- in_weight: bfloat16 [2, 1024, 4384], P('section', ('dp', 'ctx')), may hold values from -0.1875 to 0.1875
- conv_weight: bfloat16 [2, 4, 2304], P('section', None, ('dp', 'ctx')), may hold values from -3 to 3
- conv_bias: bfloat16 [2, 2304], P('section', ('dp', 'ctx')), may hold values from -1.5 to 1.5
- dt_bias: float32 [2, 32], P('section'), may hold values from -0.5 to 1.5
- a_log: float32 [2, 32], P('section'), as said below
- skip_gain: float32 [2, 32], P('section'), may hold values from 0.5 to 1.5
- gate_gain: bfloat16 [2, 2048], P('section', ('dp', 'ctx')), may hold values from 0.5 to 1.5
- out_weight: bfloat16 [2, 2048, 1024], P('section', ('dp', 'ctx')), may hold values from -0.125 to 0.125
Outputs:
- section_ends: float32 [2, 2, 2, 1024, 1024], P('section', None, 'dp', 'ctx')
- grad_norm_gain: float32 [2, 1024], P('section', ('dp', 'ctx'))
- grad_in_weight: float32 [2, 1024, 4384], P('section', ('dp', 'ctx'))
- grad_conv_weight: float32 [2, 4, 2304], P('section', None, ('dp', 'ctx'))
- grad_conv_bias: float32 [2, 2304], P('section', ('dp', 'ctx'))
- grad_dt_bias: float32 [2, 32], P('section')
- grad_a_log: float32 [2, 32], P('section')
- grad_skip_gain: float32 [2, 32], P('section')
- grad_gate_gain: float32 [2, 2048], P('section', ('dp', 'ctx'))
- grad_out_weight: float32 [2, 2048, 1024], P('section', ('dp', 'ctx'))
Inputs may be any that keep to these rules, and one draw needn't show every extreme that they name: `segments`: each sequence's document numbers start at 0, never fall and rise by one where a document starts; documents hold 60 to 800 tokens, except the last of a sequence, which may be shorter, and a sequence's single document, which holds all its tokens; for each sequence index, one micro-batch drawn from the seed holds a single document over the whole sequence; some sequence reaches the largest document number. exp(a_log) lies between 0.2 / 1024 and 0.04.
All inputs are finite; a program needn't handle non-finite values.
Results may differ from a plain program's by a relative error of at most 0.013.
Values may be sent and summed in bfloat16 or wider, within the bound.
A program may use at most 192 MiB of HBM per device.

v0:
```python
import jax
import jax.numpy as jnp
from jax import lax
from jax.sharding import PartitionSpec as P

DI = 2048
HEADS = 32
HEAD = 64
STATE = 128
XBC = 2304
PROJ = 4384


EPS = 1e-05
HIGH = lax.Precision.HIGHEST


def passed_along(block, axis, distance):
    devices = range(lax.axis_size(axis))
    route = [(i - distance, i) for i in devices if i - distance in devices]
    return lax.ppermute(block, axis, route)


def rms_scale(values):
    return values * lax.rsqrt(jnp.mean(values * values, axis=-1, keepdims=True) + EPS)


def norm_in(values, gain_vec):
    return rms_scale(values) * gain_vec


def conv_part(extended, seg_ext, conv_taps, conv_offset):
    taps_count = conv_taps.shape[0]
    length = extended.shape[0] - (taps_count - 1)
    current = seg_ext[taps_count - 1 :]
    summed = conv_offset + conv_taps[0] * extended[taps_count - 1 :]
    for offset in range(1, taps_count):
        begin_at = taps_count - 1 - offset
        shifted = extended[begin_at : begin_at + length]
        matches = seg_ext[begin_at : begin_at + length] == current
        summed = summed + conv_taps[offset] * jnp.where(matches[:, None], shifted, 0.0)
    return jax.nn.silu(summed)


def mixer_front(extended, step_raw, conv_taps, conv_offset, step_shift, a_logs, seg_ext):
    conved = conv_part(extended, seg_ext, conv_taps, conv_offset)
    inner_vals = conved[:, :DI].reshape(conved.shape[0], HEADS, HEAD)
    write_vec = conved[:, DI : DI + STATE]
    read_vec = conved[:, DI + STATE :]
    step_size = jax.nn.softplus(step_raw + step_shift)
    log_decay = -step_size * jnp.exp(a_logs)
    return (inner_vals, write_vec, read_vec, step_size, log_decay)


def block_summary(inner_vals, write_vec, step_size, log_decay, seg_block, seg_prior):
    cum_decay = jnp.cumsum(log_decay, axis=0)
    in_last = seg_block == seg_block[-1]
    tail_weight = (
        jnp.where(in_last[:, None], jnp.exp(cum_decay[-1][None, :] - cum_decay), 0.0) * step_size
    )
    local_state = jnp.einsum(
        "shp,sn->hpn", tail_weight[:, :, None] * inner_vals, write_vec, precision=HIGH
    )
    decay_tot = jnp.where(seg_block[-1] == seg_prior, jnp.exp(cum_decay[-1]), 0.0)
    return (decay_tot, local_state)


def block_output(
    inner_vals, write_vec, read_vec, step_size, log_decay, seg_block, seg_prior, skip_vec, state_in
):
    cum_decay = jnp.cumsum(log_decay, axis=0)
    block_len = seg_block.shape[0]
    order_idx = jnp.arange(block_len)
    same_doc = (seg_block[:, None] == seg_block[None, :]) & (
        order_idx[None, :] <= order_idx[:, None]
    )
    rate_rows = cum_decay.T
    decay_mat = jnp.exp(
        jnp.where(same_doc[None], rate_rows[:, :, None] - rate_rows[:, None, :], -jnp.inf)
    )
    scores = jnp.dot(read_vec, write_vec.T, precision=HIGH)
    weights = decay_mat * scores[None] * step_size.T[:, None, :]
    mixed_vals = jnp.einsum("hts,shp->thp", weights, inner_vals, precision=HIGH)
    carry_in = jnp.where((seg_block == seg_prior)[:, None], jnp.exp(cum_decay), 0.0)
    mixed_vals = mixed_vals + carry_in[:, :, None] * jnp.einsum(
        "hpn,tn->thp", state_in, read_vec, precision=HIGH
    )
    return mixed_vals + skip_vec[None, :, None] * inner_vals


def gated_output(
    inner_vals,
    write_vec,
    read_vec,
    step_size,
    log_decay,
    gate_vals,
    skip_vec,
    gain_gate,
    state_in,
    seg_block,
    seg_prior,
):
    mixed_vals = block_output(
        inner_vals,
        write_vec,
        read_vec,
        step_size,
        log_decay,
        seg_block,
        seg_prior,
        skip_vec,
        state_in,
    )
    gated = mixed_vals.reshape(mixed_vals.shape[0], DI) * jax.nn.silu(gate_vals)
    return norm_in(gated, gain_gate)


def pass_states(decay_tot, local_state):

    def advance(count_step, incoming):
        return passed_along(decay_tot[:, None, None] * incoming + local_state, "ctx", 1)

    return lax.fori_loop(0, lax.axis_size("ctx") - 1, advance, jnp.zeros_like(local_state))


def pass_grads(decay_tot, direct):

    def retreat(count_step, incoming):
        return passed_along(
            (decay_tot[:, None, None] * incoming + direct).astype(jnp.bfloat16), "ctx", -1
        ).astype(jnp.float32)

    return lax.fori_loop(0, lax.axis_size("ctx") - 1, retreat, jnp.zeros_like(direct))


def body(
    inputs,
    segments,
    cotangent,
    norm_gain,
    in_weight,
    conv_weight,
    conv_bias,
    dt_bias,
    a_log,
    skip_gain,
    gate_gain,
    out_weight,
):
    section_index = lax.axis_index("section")
    ctx_index = lax.axis_index("ctx")
    micro_count = inputs.shape[0]
    tokens = inputs.shape[2]
    model_width = inputs.shape[3]
    taps_count = conv_weight.shape[1]
    step_shift = dt_bias[0]
    a_logs = a_log[0]
    skip_vec = skip_gain[0]

    def unpack(gathered):
        return (
            gathered[0][0].astype(jnp.float32),
            gathered[1][0],
            gathered[2][0].astype(jnp.float32),
            gathered[3][0].astype(jnp.float32),
            gathered[4][0].astype(jnp.float32),
            gathered[5][0],
        )

    weights = unpack(
        (
            lax.all_gather(norm_gain, ("dp", "ctx"), axis=1, tiled=True),
            lax.all_gather(in_weight, ("dp", "ctx"), axis=1, tiled=True),
            lax.all_gather(conv_weight, ("dp", "ctx"), axis=2, tiled=True),
            lax.all_gather(conv_bias, ("dp", "ctx"), axis=1, tiled=True),
            lax.all_gather(gate_gain, ("dp", "ctx"), axis=1, tiled=True),
            lax.all_gather(out_weight, ("dp", "ctx"), axis=1, tiled=True),
        )
    )
    padded = jnp.concatenate(
        [jnp.full((micro_count, taps_count - 1), -1, jnp.int32), segments[:, 0]], axis=1
    )

    def layer_backward(grad_next, saved, is_active, layer_weights):
        gain_in, in_mat, conv_taps, conv_offset, gain_gate, out_mat = layer_weights
        layer_in, normed, projected, extended, state_in, mixed_out, seg_ext = saved
        seg_block = seg_ext[taps_count - 1 :]
        seg_prior = seg_ext[taps_count - 2]
        grad_out = jnp.where(is_active, grad_next, 0.0).astype(jnp.bfloat16)
        grad_mixed = lax.cond(
            is_active,
            lambda: lax.dot_general(
                grad_out, out_mat, (((1,), (1,)), ((), ())), preferred_element_type=jnp.float32
            ),
            lambda: jnp.zeros((tokens, DI), jnp.float32),
        )
        gate_vals = projected[:, :DI]
        step_raw = projected[:, DI + XBC :]

        def front_local(ext_vals, raw_vals, taps_vals, offset_vals, shift_vals, log_vals):
            return mixer_front(
                ext_vals, raw_vals, taps_vals, offset_vals, shift_vals, log_vals, seg_ext
            )

        pieces, front_pull = jax.vjp(
            front_local,
            extended.astype(jnp.float32),
            step_raw,
            conv_taps,
            conv_offset,
            step_shift,
            a_logs,
        )

        def output_local(
            inner_vals,
            write_vec,
            read_vec,
            step_size,
            log_decay,
            gate_part,
            skip_part,
            gain_part,
            state_part,
        ):
            return gated_output(
                inner_vals,
                write_vec,
                read_vec,
                step_size,
                log_decay,
                gate_part,
                skip_part,
                gain_part,
                state_part,
                seg_block,
                seg_prior,
            )

        unused_out, output_pull = jax.vjp(
            output_local,
            pieces[0],
            pieces[1],
            pieces[2],
            pieces[3],
            pieces[4],
            gate_vals,
            skip_vec,
            gain_gate,
            state_in,
        )
        (
            grad_inner,
            grad_write,
            grad_read,
            grad_step,
            grad_logdec,
            grad_gate,
            grad_skip,
            grad_gaingate,
            grad_state,
        ) = output_pull(grad_mixed)

        def summary_local(inner_vals, write_vec, step_size, log_decay):
            return block_summary(inner_vals, write_vec, step_size, log_decay, seg_block, seg_prior)

        summary_vals, summary_pull = jax.vjp(
            summary_local, pieces[0], pieces[1], pieces[3], pieces[4]
        )
        onward = pass_grads(summary_vals[0], grad_state)
        back_inner, back_write, back_step, back_logdec = summary_pull(
            (jnp.sum(onward * state_in, axis=(1, 2)), onward)
        )
        grad_ext, grad_raw, grad_taps, grad_offset, grad_shift, grad_alog = front_pull(
            (
                grad_inner + back_inner,
                grad_write + back_write,
                grad_read,
                grad_step + back_step,
                grad_logdec + back_logdec,
            )
        )
        returned = passed_along(grad_ext[: taps_count - 1], "ctx", -1)
        grad_conv = grad_ext[taps_count - 1 :] + jnp.concatenate(
            [jnp.zeros((tokens - taps_count + 1, XBC), jnp.float32), returned], axis=0
        )
        grad_proj = jnp.where(
            is_active, jnp.concatenate([grad_gate, grad_conv, grad_raw], axis=1), 0.0
        ).astype(jnp.bfloat16)
        grad_normed = lax.cond(
            is_active,
            lambda: lax.dot_general(
                grad_proj, in_mat, (((1,), (1,)), ((), ())), preferred_element_type=jnp.float32
            ),
            lambda: jnp.zeros((tokens, model_width), jnp.float32),
        )
        unused_norm, norm_pull = jax.vjp(norm_in, layer_in.astype(jnp.float32), gain_in)
        grad_layer, grad_gainin = norm_pull(grad_normed)
        small_grads = (grad_gainin, grad_taps, grad_offset, grad_gaingate)
        return (
            grad_next + grad_layer,
            small_grads,
            (grad_shift, grad_alog, grad_skip),
            (normed, grad_proj, mixed_out, grad_out),
        )

    received = jnp.zeros((tokens, model_width), jnp.bfloat16)
    results = []
    kept_all = []
    for tick_index in range(micro_count + 1):
        own_input = inputs[min(tick_index, micro_count - 1), 0]
        layer_in = jnp.where(section_index == 0, own_input, received)
        micro_index = jnp.clip(tick_index - section_index, 0, micro_count - 1)
        is_active = jnp.where(section_index == 0, tick_index < micro_count, tick_index >= 1)
        seg_row = lax.dynamic_index_in_dim(padded, micro_index, 0, keepdims=False)
        layer_seg_ext = lax.dynamic_slice_in_dim(
            seg_row, ctx_index * tokens, tokens + taps_count - 1
        )
        (
            layer_gain_in,
            layer_in_mat,
            layer_conv_taps,
            layer_conv_offset,
            layer_gain_gate,
            layer_out_mat,
        ) = weights
        layer_seg_block = layer_seg_ext[taps_count - 1 :]
        layer_seg_prior = layer_seg_ext[taps_count - 2]
        start_vals = layer_in.astype(jnp.float32)
        layer_normed = norm_in(start_vals, layer_gain_in).astype(jnp.bfloat16)
        layer_projected = lax.cond(
            is_active,
            lambda: jnp.dot(layer_normed, layer_in_mat, preferred_element_type=jnp.float32),
            lambda: jnp.zeros((tokens, PROJ), jnp.float32),
        )
        layer_gate_vals = layer_projected[:, :DI]
        raw_conv = layer_projected[:, DI : DI + XBC].astype(jnp.bfloat16)
        layer_step_raw = layer_projected[:, DI + XBC :]
        before = passed_along(raw_conv[tokens - taps_count + 1 :], "ctx", 1)
        layer_extended = jnp.concatenate([before, raw_conv], axis=0)
        layer_pieces = mixer_front(
            layer_extended.astype(jnp.float32),
            layer_step_raw,
            layer_conv_taps,
            layer_conv_offset,
            step_shift,
            a_logs,
            layer_seg_ext,
        )
        decay_tot, local_state = block_summary(
            layer_pieces[0],
            layer_pieces[1],
            layer_pieces[3],
            layer_pieces[4],
            layer_seg_block,
            layer_seg_prior,
        )
        layer_state_in = pass_states(decay_tot, local_state)
        layer_mixed_out = gated_output(
            layer_pieces[0],
            layer_pieces[1],
            layer_pieces[2],
            layer_pieces[3],
            layer_pieces[4],
            layer_gate_vals,
            skip_vec,
            layer_gain_gate,
            layer_state_in,
            layer_seg_block,
            layer_seg_prior,
        ).astype(jnp.bfloat16)
        branch = lax.cond(
            is_active,
            lambda: jnp.dot(layer_mixed_out, layer_out_mat, preferred_element_type=jnp.float32),
            lambda: jnp.zeros((tokens, model_width), jnp.float32),
        )
        result = start_vals + branch
        saved = (
            layer_in,
            layer_normed,
            layer_projected,
            layer_extended,
            layer_state_in,
            layer_mixed_out,
            layer_seg_ext,
        )
        results.append(result)
        kept_all.append(saved)
        if tick_index < micro_count:
            received = passed_along(result.astype(jnp.bfloat16), "section", 1)
    weights = unpack(
        (
            lax.all_gather(norm_gain, ("dp", "ctx"), axis=1, tiled=True),
            lax.all_gather(in_weight, ("dp", "ctx"), axis=1, tiled=True),
            lax.all_gather(conv_weight, ("dp", "ctx"), axis=2, tiled=True),
            lax.all_gather(conv_bias, ("dp", "ctx"), axis=1, tiled=True),
            lax.all_gather(gate_gain, ("dp", "ctx"), axis=1, tiled=True),
            lax.all_gather(out_weight, ("dp", "ctx"), axis=1, tiled=True),
        )
    )
    small_sums = (
        jnp.zeros(weights[0].shape, jnp.float32),
        jnp.zeros(weights[2].shape, jnp.float32),
        jnp.zeros(weights[3].shape, jnp.float32),
        jnp.zeros(weights[4].shape, jnp.float32),
    )
    head_sums = tuple((jnp.zeros(step_shift.shape, jnp.float32) for repeat_idx in range(3)))
    returned_grad = jnp.zeros((tokens, model_width), jnp.bfloat16)
    grad_inputs = []
    row_parts = []
    for tick_index in range(micro_count + 1):
        lower_saved = kept_all[max(tick_index - 1, 0)]
        upper_saved = kept_all[min(tick_index + 1, micro_count)]
        saved = jax.tree.map(
            lambda lower_val, upper_val: jnp.where(section_index == 0, lower_val, upper_val),
            lower_saved,
            upper_saved,
        )
        target = cotangent[min(tick_index, micro_count - 1), 0].astype(jnp.float32)
        grad_next = jnp.where(section_index == 1, target, returned_grad.astype(jnp.float32))
        is_active = jnp.where(section_index == 1, tick_index < micro_count, tick_index >= 1)
        grad_input, small_grads, head_grads, rows_kept = layer_backward(
            grad_next, saved, is_active, weights
        )
        small_sums = jax.tree.map(
            lambda running, update: running + jnp.where(is_active, update, 0.0),
            small_sums,
            small_grads,
        )
        head_sums = jax.tree.map(
            lambda running, update: running + jnp.where(is_active, update, 0.0),
            head_sums,
            head_grads,
        )
        row_parts.append(rows_kept)
        grad_inputs.append(grad_input)
        if tick_index < micro_count:
            returned_grad = passed_along(grad_input.astype(jnp.bfloat16), "section", -1)
    normed_rows = jnp.concatenate([part_item[0] for part_item in row_parts], axis=0)
    proj_rows = jnp.concatenate([part_item[1] for part_item in row_parts], axis=0)
    mixed_rows = jnp.concatenate([part_item[2] for part_item in row_parts], axis=0)
    branch_rows = jnp.concatenate([part_item[3] for part_item in row_parts], axis=0)
    grad_inmat = lax.dot_general(
        normed_rows, proj_rows, (((0,), (0,)), ((), ())), preferred_element_type=jnp.float32
    )
    grad_outmat = lax.dot_general(
        mixed_rows, branch_rows, (((0,), (0,)), ((), ())), preferred_element_type=jnp.float32
    )
    taps_turned = jnp.transpose(small_sums[1])
    owned = (
        lax.psum_scatter(small_sums[0][None], ("dp", "ctx"), scatter_dimension=1, tiled=True),
        lax.psum_scatter(grad_inmat[None], ("dp", "ctx"), scatter_dimension=1, tiled=True),
        lax.psum_scatter(taps_turned[None], ("dp", "ctx"), scatter_dimension=1, tiled=True),
        lax.psum_scatter(small_sums[2][None], ("dp", "ctx"), scatter_dimension=1, tiled=True),
        lax.psum_scatter(small_sums[3][None], ("dp", "ctx"), scatter_dimension=1, tiled=True),
        lax.psum_scatter(grad_outmat[None], ("dp", "ctx"), scatter_dimension=1, tiled=True),
    )
    head_totals = lax.psum(
        (head_sums[0][None], head_sums[1][None], head_sums[2][None]), ("dp", "ctx")
    )
    ends_rows = [
        jnp.where(section_index == 0, grad_inputs[micro_index + 1], results[micro_index + 1])
        for micro_index in range(micro_count)
    ]
    section_ends = jnp.stack(ends_rows)[None, :, None]
    conv_owned = jnp.transpose(owned[2], (0, 2, 1))
    return (
        section_ends,
        owned[0],
        owned[1],
        conv_owned,
        owned[3],
        head_totals[0],
        head_totals[1],
        head_totals[2],
        owned[4],
        owned[5],
    )


def solution(mesh):
    return jax.shard_map(
        body,
        mesh=mesh,
        in_specs=(
            P(None, "dp", "ctx", None),
            P(None, "dp", None),
            P(None, "dp", "ctx", None),
            P("section", ("dp", "ctx")),
            P("section", ("dp", "ctx"), None),
            P("section", None, ("dp", "ctx")),
            P("section", ("dp", "ctx")),
            P("section", None),
            P("section", None),
            P("section", None),
            P("section", ("dp", "ctx")),
            P("section", ("dp", "ctx"), None),
        ),
        out_specs=(
            P("section", None, "dp", "ctx", None),
            P("section", ("dp", "ctx")),
            P("section", ("dp", "ctx"), None),
            P("section", None, ("dp", "ctx")),
            P("section", ("dp", "ctx")),
            P("section", None),
            P("section", None),
            P("section", None),
            P("section", ("dp", "ctx")),
            P("section", ("dp", "ctx"), None),
        ),
        check_vma=False,
    )
```

profile of v0, /device:TPU:0, one launch (start us, length us, event | category | flops | bytes accessed | tf_op | source)
XLA Modules:
  0.0 1869.6 jit_solution(3553106564330517667)
XLA Ops:
  28.1 36.6 %all-reduce.47 = (bf16[1024]{0:T(1024)(128)(2,1)S(1)}, bf16[2304]{0:T(1024)(128)(2,1)S(1)}) all-reduce(bf16[1024]{0:T(1024)(128)(2,1)S(1)} %dynamic-update-slice.1, bf16[2304]{0:T(1024)(128)(2,1)S(1)} %dynamic-update-slice), channel_id=1, replica_groups=mesh['section'=2,'dp'=2,'ctx'=8] {'dp','ctx'}, use_global_device_ids=true, to_apply=%add.44 | all-reduce | flops 3328 | bytes 13312
  65.4 37.1 %all_gather.25 = bf16[1,4,2304]{1,0,2:T(2,128)(2,1)S(1)} all-gather(bf16[1,4,144]{1,0,2:T(2,128)(2,1)S(1)} %copy.538), channel_id=1, replica_groups=mesh['section'=2,'dp'=2,'ctx'=8] {'dp','ctx'}, dimensions={2}, use_global_device_ids=true | all-gather | bytes 19584 | tf_op jit(solution)/shard_map/all_gather | solution.py:396
  103.8 17.4 all_gather.28
  124.0 47.9 %slice_reduce_fusion.3 = (f32[2304]{0:T(1024)S(1)}, f32[2304]{0:T(1024)S(1)}, f32[2304]{0:T(1024)S(1)}, f32[2304]{0:T(1024)S(1)}) fusion(f32[1,4,2304]{1,0,2:T(1,128)S(1)} %convert_element_type.160), kind=kLoop, calls=%fused_computation.178 | loop fusion | bytes 73728 | tf_op jit(solution)/shard_map/jvp()/slice | solution.py:36
  171.9 7.5 conditional.8
  172.2 7.3 fusion.477
  201.3 100.8 %while.63 = (s32[]{:T(128)}, f32[32,64,128]{2,1,0:T(8,128)S(1)}, f32[32]{0:T(128)S(1)}, f32[32,64,128]{2,1,0:T(8,128)S(1)}, s32[]{:T(128)}) while((s32[]{:T(128)}, f32[32,64,128]{2,1,0:T(8,128)S(1)}, f32[32]{0:T(128)S(1)}, f32[32,64,128]{2,1,0:T(8,128)S(1)}, s32[]{:T(128)}) %tuple.395), condition=%wide.region_5.6_spmd, body=%wide.region_4.5_spmd.sunk | while | flops 524290 | bytes 7340261 | solution.py:124
  206.8 11.7 collective-permute-start
  220.9 13.9 collective-permute-start
  237.2 13.9 collective-permute-start
  253.5 13.9 collective-permute-start
  269.7 13.9 collective-permute-start
  286.0 13.9 collective-permute-start
  311.2 12.7 collective-permute-start.7
  328.0 8.3 fusion.475
  338.7 13.8 collective-permute-start.8
  364.7 103.9 %while.64 = (s32[]{:T(128)}, f32[32,64,128]{2,1,0:T(8,128)S(1)}, f32[32]{0:T(128)S(1)}, f32[32,64,128]{2,1,0:T(8,128)S(1)}, s32[]{:T(128)}) while((s32[]{:T(128)}, f32[32,64,128]{2,1,0:T(8,128)S(1)}, f32[32]{0:T(128)S(1)}, f32[32,64,128]{2,1,0:T(8,128)S(1)}, s32[]{:T(128)}) %tuple.398), condition=%wide.region_13.15_spmd, body=%wide.region_12.14_spmd.sunk | while | flops 524290 | bytes 7340261 | solution.py:124
  371.7 13.2 collective-permute-start.1
  387.3 13.9 collective-permute-start.1
  403.6 13.9 collective-permute-start.1
  419.9 13.9 collective-permute-start.1
  436.2 13.9 collective-permute-start.1
  452.5 13.9 collective-permute-start.1
  509.7 14.4 collective-permute-start.12
  562.3 121.5 %while.65 = (s32[]{:T(128)}, f32[32,64,128]{2,1,0:T(8,128)}, f32[32]{0:T(128)S(1)}, f32[32,64,128]{2,1,0:T(8,128)}, s32[]{:T(128)}) while((s32[]{:T(128)}, f32[32,64,128]{2,1,0:T(8,128)}, f32[32]{0:T(128)S(1)}, f32[32,64,128]{2,1,0:T(8,128)}, s32[]{:T(128)}) %tuple.456), condition=%wide.region_41.43_spmd, body=%wide.region_40.42_spmd.sunk | while | flops 524290 | bytes 7340261 | solution.py:124
  574.1 12.3 collective-permute-start.2
  590.7 14.8 collective-permute-start.2
  609.9 14.8 collective-permute-start.2
  629.0 14.8 collective-permute-start.2
  648.1 14.8 collective-permute-start.2
  667.2 14.8 collective-permute-start.2
  712.4 105.2 %while.66 = (s32[]{:T(128)}, f32[32,64,128]{2,1,0:T(8,128)S(1)}, f32[32]{0:T(128)S(1)}, f32[32,64,128]{2,1,0:T(8,128)}, s32[]{:T(128)}, /*index=5*/s32[]{:T(128)}) while((s32[]{:T(128)}, f32[32,64,128]{2,1,0:T(8,128)S(1)}, f32[32]{0:T(128)S(1)}, f32[32,64,128]{2,1,0:T(8,128)}, s32[]{:T(128)}, /*index=5*/s32[]{:T(128)}) %tuple.406), condition=%wide.region_20.22_spmd.clone, body=%wide.region_19.21_spmd.clone.sunk | while | flops 1310723 | bytes 6291703 | solution.py:134
  715.9 14.3 collective-permute-done.3
  734.8 10.3 collective-permute-done.3
  749.7 9.5 collective-permute-done.3
  763.9 9.5 collective-permute-done.3
  778.1 9.5 collective-permute-done.3
  792.3 9.5 collective-permute-done.3
  806.4 9.5 collective-permute-done.3
  890.2 12.9 collective-permute-done.10
  912.6 92.4 %while.67 = (s32[]{:T(128)}, f32[32,64,128]{2,1,0:T(8,128)S(1)}, f32[32]{0:T(128)S(1)}, f32[32,64,128]{2,1,0:T(8,128)S(1)}, s32[]{:T(128)}, /*index=5*/s32[]{:T(128)}) while((s32[]{:T(128)}, f32[32,64,128]{2,1,0:T(8,128)S(1)}, f32[32]{0:T(128)S(1)}, f32[32,64,128]{2,1,0:T(8,128)S(1)}, s32[]{:T(128)}, ...), condition=%wide.region_46.48_spmd.clone, body=%wide.region_45.47_spmd.clone.sunk | while | flops 1310723 | bytes 6291703 | solution.py:134
  914.9 9.3 collective-permute-done.4
  927.6 11.1 collective-permute-done.4
  942.2 9.5 collective-permute-done.4
  955.2 9.5 collective-permute-done.4
  968.1 9.5 collective-permute-done.4
  981.1 9.5 collective-permute-done.4
  994.1 9.5 collective-permute-done.4
  1058.2 7.6 fusion.288
  1085.4 92.5 %while.68 = (s32[]{:T(128)}, f32[32,64,128]{2,1,0:T(8,128)S(1)}, f32[32]{0:T(128)S(1)}, f32[32,64,128]{2,1,0:T(8,128)S(1)}, s32[]{:T(128)}, /*index=5*/s32[]{:T(128)}) while((s32[]{:T(128)}, f32[32,64,128]{2,1,0:T(8,128)S(1)}, f32[32]{0:T(128)S(1)}, f32[32,64,128]{2,1,0:T(8,128)S(1)}, s32[]{:T(128)}, ...), condition=%wide.region_65.67_spmd.clone, body=%wide.region_64.66_spmd.clone.sunk | while | flops 1310723 | bytes 6291703 | solution.py:134
  1087.7 9.6 collective-permute-done.5
  1100.7 11.1 collective-permute-done.5
  1115.3 9.5 collective-permute-done.5
  1128.3 9.5 collective-permute-done.5
  1141.2 9.5 collective-permute-done.5
  1154.2 9.5 collective-permute-done.5
  1167.2 9.5 collective-permute-done.5
  1242.7 12.4 convolution_bitcast_fusion
  1255.1 37.6 %copy.636 = f32[1,1024,4384]{2,0,1:T(1,128)} copy(f32[1,1024,4384]{1,2,0:T(8,128)} %convolution_bitcast_fusion) | data formatting | bytes 35913728 | tf_op jit(solution)/shard_map/broadcast_in_dim | solution.py:453
  1302.9 38.5 %all-reduce.46 = (f32[1,32]{1,0:T(1,128)}, f32[1,32]{1,0:T(1,128)}, f32[1,32]{1,0:T(1,128)}) all-reduce(f32[1,32]{1,0:T(1,128)S(1)} %fusion.422, f32[1,32]{1,0:T(1,128)S(1)} %fusion.402, f32[1,32]{1,0:T(1,128)S(1)} %fusion.421), channel_id=1, replica_groups=mesh['section'=2,'dp'=2,'ctx'=8] {'dp','ctx'}, use_global_device_ids=true, to_apply=%region_107.109 | all-reduce | flops 96 | bytes 768 | tf_op jit(solution)/shard_map/psum | solution.py:459
  1346.5 20.7 %reduce-scatter.16.cloned.1.call-done = f32[64,1]{1,0:T(8,128)} async-done(((f32[1024,1]{1,0:T(8,128)}), f32[64,1]{1,0:T(8,128)}) %reduce-scatter.16.cloned.1.call-update) | async-done | bytes 272
  1368.6 59.3 %reduce-scatter.18.cloned.1.call-done = f32[144,4]{1,0:T(8,128)} async-done(((f32[2304,4]{1,0:T(8,128)}), f32[144,4]{1,0:T(8,128)}) %reduce-scatter.18.cloned.1.call-update) | async-done | bytes 2320
  1429.4 323.9 %all-reduce.50.cloned.1.call-done = f32[1,1024,4384]{2,0,1:T(1,128)} async-done(((f32[1,1024,4384]{2,0,1:T(1,128)}), f32[1,1024,4384]{2,0,1:T(1,128)}) %all-reduce.50.cloned.1.call-update) | async-done | bytes 17956880
  1755.8 106.5 %reduce-scatter.14.cloned.1.call-done = f32[1,128,1024]{2,1,0:T(8,128)} async-done(((f32[1,2048,1024]{2,1,0:T(8,128)}), f32[1,128,1024]{2,1,0:T(8,128)}) %reduce-scatter.14.cloned.1.call-update) | async-done | bytes 524304 | tf_op jit(solution)/shard_map/reduce_scatter | solution.py:457
  (1047 shorter events, 580.6 us)
Async XLA Ops:
  7.2 164.7 %all-gather.3.cloned.1.call-start = ((), (), s32[]{:S(2)}) async-start(), calls=%async_computation.5 | async-start | bytes 9748480 | tf_op jit(solution)/shard_map/all_gather | solution.py:174
  8.0 300.1 %all-gather.5.cloned.1.call-start = ((), (), s32[]{:S(2)}) async-start(), calls=%async_computation.6 | async-start | bytes 4456448 | tf_op jit(solution)/shard_map/all_gather | solution.py:178
  8.7 1332.7 %reduce-scatter.22.cloned.1.call-start = ((), (), s32[]{:S(2)}) async-start(), calls=%async_computation.11 | async-start | bytes 1114112
  9.6 314.3 %copy-start.194 = (s32[1,131]{1,0:T(1,128)}, s32[1,131]{1,0:T(1,128)S(1)}, u32[]{:S(2)}) copy-start(s32[1,131]{1,0:T(1,128)S(1)} %get-tuple-element.618) | copy-start | bytes 1576
  20.4 315.9 %copy-start.184 = (f32[32]{0:T(128)}, f32[32]{0:T(128)S(1)}, u32[]{:S(2)}) copy-start(f32[32]{0:T(128)S(1)} %exponential_bitcast_fusion) | copy-start | bytes 388
  65.3 289.8 %copy-start.109 = (f32[2304]{0:T(1024)}, f32[2304]{0:T(1024)S(1)}, u32[]{:S(2)}) copy-start(f32[2304]{0:T(1024)S(1)} %add.808) | copy-start | bytes 27652
  182.9 6.9 collective-permute-start.6
  201.5 5.1 collective-permute-start
  206.8 13.9 collective-permute-start
  220.9 16.1 collective-permute-start
  237.2 16.1 collective-permute-start
  253.5 16.1 collective-permute-start
  269.7 16.1 collective-permute-start
  286.0 16.1 collective-permute-start
  311.2 15.3 collective-permute-start.7
  338.7 15.2 collective-permute-start.8
  364.9 6.7 collective-permute-start.1
  371.7 15.5 collective-permute-start.1
  387.3 16.1 collective-permute-start.1
  403.6 16.1 collective-permute-start.1
  419.9 16.1 collective-permute-start.1
  436.2 16.1 collective-permute-start.1
  452.5 16.1 collective-permute-start.1
  476.2 10.2 collective-permute-start.11
  509.7 30.3 %collective-permute-start.12 = (bf16[3,2304]{1,0:T(4,128)(2,1)}, bf16[3,2304]{1,0:T(4,128)(2,1)}, u32[]{:S(2)}, u32[]{:S(2)}) collective-permute-start(bf16[3,2304]{1,0:T(4,128)(2,1)} %copy.581), channel_id=1, source_target_pairs={{0,1},{1,2},{2,3},{3,4},{4,5},{5,6},{6,7},{8,9},{9,10},{10,11},{11... | collective-permute-start | bytes 41480 | tf_op jit(solution)/shard_map/ppermute | solution.py:21
  538.6 160.7 %copy-start.113 = (f32[32,128]{1,0:T(8,128)}, f32[32,128]{1,0:T(8,128)S(1)}, u32[]{:S(2)}) copy-start(f32[32,128]{1,0:T(8,128)S(1)} %copy.609) | copy-start | bytes 49156
  565.0 6.4 collective-permute-start.2
  574.1 14.0 collective-permute-start.2
  590.7 16.4 collective-permute-start.2
  609.9 16.4 collective-permute-start.2
  629.0 16.4 collective-permute-start.2
  648.1 16.4 collective-permute-start.2
  667.2 16.4 collective-permute-start.2
  714.6 15.5 collective-permute-start.3
  733.5 11.6 collective-permute-start.3
  748.4 10.8 collective-permute-start.3
  762.6 10.8 collective-permute-start.3
  776.8 10.8 collective-permute-start.3
  791.0 10.8 collective-permute-start.3
  805.2 10.8 collective-permute-start.3
  849.8 24.0 %collective-permute-start.9 = (f32[3,2304]{1,0:T(4,128)}, f32[3,2304]{1,0:T(4,128)}, u32[]{:S(2)}, u32[]{:S(2)}) collective-permute-start(f32[3,2304]{1,0:T(4,128)} %copy.568), channel_id=1, source_target_pairs={{1,0},{2,1},{3,2},{4,3},{5,4},{6,5},{7,6},{9,8},{10,9},{11,10},{12... | collective-permute-start | bytes 82952 | tf_op jit(solution)/shard_map/ppermute | solution.py:21
  885.3 17.9 collective-permute-start.10
  913.6 10.6 collective-permute-start.4
  926.3 12.4 collective-permute-start.4
  940.9 10.8 collective-permute-start.4
  953.9 10.8 collective-permute-start.4
  966.9 10.8 collective-permute-start.4
  979.8 10.8 collective-permute-start.4
  992.8 10.8 collective-permute-start.4
  1033.2 20.6 %collective-permute-start.13 = (f32[3,2304]{1,0:T(4,128)}, f32[3,2304]{1,0:T(4,128)}, u32[]{:S(2)}, u32[]{:S(2)}) collective-permute-start(f32[3,2304]{1,0:T(4,128)} %copy.600), channel_id=1, source_target_pairs={{1,0},{2,1},{3,2},{4,3},{5,4},{6,5},{7,6},{9,8},{10,9},{11,10},{12... | collective-permute-start | bytes 82952 | tf_op jit(solution)/shard_map/ppermute | solution.py:21
  1067.7 8.3 collective-permute-start.14
  1086.4 10.8 collective-permute-start.5
  1099.4 12.4 collective-permute-start.5
  1114.0 10.8 collective-permute-start.5
  1127.0 10.8 collective-permute-start.5
  1140.0 10.8 collective-permute-start.5
  1152.9 10.8 collective-permute-start.5
  1165.9 10.8 collective-permute-start.5
  1186.1 156.8 %reduce-scatter.20.cloned.1.call-start = ((), (), s32[]{:S(2)}) async-start(), calls=%async_computation.10 | async-start | bytes 1253376
  1216.3 9.9 collective-permute-start.15
  1225.3 141.9 %reduce-scatter.16.cloned.1.call-start = ((), (), s32[]{:S(2)}) async-start(), calls=%async_computation.8 | async-start | bytes 557056
  1238.2 189.7 %reduce-scatter.18.cloned.1.call-start = ((), (), s32[]{:S(2)}) async-start(), calls=%async_computation.9 | async-start | bytes 1253376
  1242.3 511.0 %all-reduce.50.cloned.1.call-start = ((), (), s32[]{:S(2)}) async-start(), calls=%async_computation.12 | async-start | bytes 36700160
  1292.7 569.6 %reduce-scatter.14.cloned.1.call-start = ((), (), s32[]{:S(2)}) async-start(), calls=%async_computation.7 | async-start | bytes 8912896 | tf_op jit(solution)/shard_map/reduce_scatter | solution.py:457
  (283 other events, 1766.6 us)
Sparse Core Ops, SparseCore 0:
  10.4 92.0 all-gather.2
  104.7 49.6 all-gather.4
  1186.2 61.4 reduce-scatter.21
  1251.6 56.9 reduce-scatter.19
  1312.4 54.8 reduce-scatter.15
  1370.7 57.0 reduce-scatter.17
  1431.8 321.5 all-reduce.49
  1757.9 104.3 reduce-scatter.13
where the time goes:
time: 1890 us; the launch traced here: 1870 us
  waiting for transfers between devices  778 us (41%)
  starting transfers between devices  342 us (18%)
  other arithmetic  247 us (13%)
  local copies, waits for them, and re-layouts  183 us (10%)
  matrix products  160 us (8%)
  blocking collectives  130 us (7%)
  between operations  28 us (1%)
    unnamed x13, waiting for transfers between devices  405 us
    ppermute x52, starting transfers between devices, passed_along(): return lax.ppermute(block, axis, route)  342 us
    ppermute x52, waiting for transfers between devices, passed_along(): return lax.ppermute(block, axis, route)  266 us
    reduce_scatter x1, waiting for transfers between devices, body(): lax.psum_scatter(grad_outmat[None], ('dp', 'ctx'), scatter_dimension=1, t...  107 us
    dot_general x12, matrix products, block_output(): mixed_vals = jnp.einsum('hts,shp->thp', weights, inner_vals, precision=HIGH)  49.9 us
    slice x1, local copies, waits for them, and re-layouts, conv_part(): summed = conv_offset + conv_taps[0] * extended[taps_count - 1:]  47.9 us
    psum x1, blocking collectives, body(): lax.psum((head_sums[0][None], head_sums[1][None], head_sums[2][None]), ('...  38.5 us
  transfers between devices with their start and end apart: 60, of which 49 were waited for; matrix products, arithmetic and copies ran while one was open for 16% of the time, Pallas kernels for 0%

commit v1 on v0

--- a/solution.py
+++ b/solution.py
@@ -116,22 +116,52 @@
     return norm_in(gated, gain_gate)
 
 
-def pass_states(decay_tot, local_state):
-
-    def advance(count_step, incoming):
-        return passed_along(decay_tot[:, None, None] * incoming + local_state, "ctx", 1)
-
-    return lax.fori_loop(0, lax.axis_size("ctx") - 1, advance, jnp.zeros_like(local_state))
-
-
-def pass_grads(decay_tot, direct):
-
-    def retreat(count_step, incoming):
-        return passed_along(
-            (decay_tot[:, None, None] * incoming + direct).astype(jnp.bfloat16), "ctx", -1
-        ).astype(jnp.float32)
-
-    return lax.fori_loop(0, lax.axis_size("ctx") - 1, retreat, jnp.zeros_like(direct))
+def split_three(values):
+    high = lax.reduce_precision(values, 8, 7)
+    rest = values - high
+    middle = lax.reduce_precision(rest, 8, 7)
+    last = lax.reduce_precision(rest - middle, 8, 7)
+    return [part.astype(jnp.bfloat16) for part in (high, middle, last)]
+
+
+def chain_weights(decays, me, step):
+    count = decays.shape[0]
+    running = jnp.ones(decays.shape[1:], jnp.float32)
+    order = range(count - 1, -1, -1) if step > 0 else range(count)
+    found = [None] * count
+    for block in order:
+        ahead = block < me if step > 0 else block > me
+        found[block] = jnp.where(ahead, running, 0.0)
+        running = jnp.where(ahead, running * decays[block], running)
+    return jnp.stack(found)
+
+
+def gather_states(decay_tot, local_state):
+    heads, channels, width = local_state.shape
+    row = jnp.concatenate(split_three(decay_tot))
+    row = jnp.pad(row, (0, width - row.shape[0]))[None]
+    row = jnp.pad(row, ((0, 15), (0, 0)))
+    rows = jnp.concatenate([local_state.reshape(heads * channels, width).astype(jnp.bfloat16), row])
+    every = lax.all_gather(rows, "ctx", axis=0, tiled=False)
+    coded = every[:, heads * channels, : 3 * heads].astype(jnp.float32)
+    decays = coded[:, :heads] + (coded[:, heads : 2 * heads] + coded[:, 2 * heads :])
+    factors = chain_weights(decays, lax.axis_index("ctx"), 1)
+    states = every[:, : heads * channels].reshape(-1, heads, channels, width)
+    return decays, jnp.sum(factors[:, :, None, None] * states.astype(jnp.float32), axis=0)
+
+
+def gather_grads(decays, direct):
+    heads, channels, width = direct.shape
+    rows = direct.reshape(heads * channels, width).astype(jnp.bfloat16)
+    every = lax.all_gather(rows, "ctx", axis=0, tiled=False)
+    factors = chain_weights(decays, lax.axis_index("ctx"), -1)
+    states = every.reshape(-1, heads, channels, width)
+    return jnp.sum(factors[:, :, None, None] * states.astype(jnp.float32), axis=0)
+
+
+def pack_small(pieces, width):
+    packed = jnp.concatenate(pieces, axis=-1)
+    return jnp.pad(packed, [(0, 0)] * (packed.ndim - 1) + [(0, width - packed.shape[-1])])
 
 
 def body(
@@ -158,25 +188,28 @@
     a_logs = a_log[0]
     skip_vec = skip_gain[0]
 
-    def unpack(gathered):
-        return (
-            gathered[0][0].astype(jnp.float32),
-            gathered[1][0],
-            gathered[2][0].astype(jnp.float32),
-            gathered[3][0].astype(jnp.float32),
-            gathered[4][0].astype(jnp.float32),
-            gathered[5][0],
-        )
-
-    weights = unpack(
-        (
-            lax.all_gather(norm_gain, ("dp", "ctx"), axis=1, tiled=True),
-            lax.all_gather(in_weight, ("dp", "ctx"), axis=1, tiled=True),
-            lax.all_gather(conv_weight, ("dp", "ctx"), axis=2, tiled=True),
-            lax.all_gather(conv_bias, ("dp", "ctx"), axis=1, tiled=True),
-            lax.all_gather(gate_gain, ("dp", "ctx"), axis=1, tiled=True),
-            lax.all_gather(out_weight, ("dp", "ctx"), axis=1, tiled=True),
-        )
+    both = ("dp", "ctx")
+    shards = lax.axis_size("dp") * lax.axis_size("ctx")
+    gain_len, gate_len = norm_gain.shape[1], gate_gain.shape[1]
+    conv_len = conv_bias.shape[1]
+    small_len = gain_len + gate_len + (taps_count + 1) * conv_len
+    small_width = -(-small_len // 1024) * 1024
+    own_small = pack_small(
+        [norm_gain[0], gate_gain[0], conv_bias[0], conv_weight[0].reshape(-1)], small_width
+    )
+    small_all = lax.all_gather(
+        own_small.reshape(small_width // 128, 128), both, axis=0, tiled=True
+    )
+    small_all = small_all.reshape(shards, small_width).astype(jnp.float32)
+    marks = (gain_len, gain_len + gate_len, gain_len + gate_len + conv_len, small_len)
+    all_taps = small_all[:, marks[2] : marks[3]].reshape(shards, taps_count, conv_len)
+    weights = (
+        small_all[:, : marks[0]].reshape(-1),
+        lax.all_gather(in_weight, both, axis=1, tiled=True)[0],
+        jnp.transpose(all_taps, (1, 0, 2)).reshape(taps_count, -1),
+        small_all[:, marks[1] : marks[2]].reshape(-1),
+        small_all[:, marks[0] : marks[1]].reshape(-1),
+        lax.all_gather(out_weight, both, axis=1, tiled=True)[0],
     )
     padded = jnp.concatenate(
         [jnp.full((micro_count, taps_count - 1), -1, jnp.int32), segments[:, 0]], axis=1
@@ -184,7 +217,7 @@
 
     def layer_backward(grad_next, saved, is_active, layer_weights):
         gain_in, in_mat, conv_taps, conv_offset, gain_gate, out_mat = layer_weights
-        layer_in, normed, projected, extended, state_in, mixed_out, seg_ext = saved
+        layer_in, normed, projected, extended, state_in, mixed_out, seg_ext, decays = saved
         seg_block = seg_ext[taps_count - 1 :]
         seg_prior = seg_ext[taps_count - 2]
         grad_out = jnp.where(is_active, grad_next, 0.0).astype(jnp.bfloat16)
@@ -268,7 +301,7 @@
         summary_vals, summary_pull = jax.vjp(
             summary_local, pieces[0], pieces[1], pieces[3], pieces[4]
         )
-        onward = pass_grads(summary_vals[0], grad_state)
+        onward = gather_grads(decays, grad_state)
         back_inner, back_write, back_step, back_logdec = summary_pull(
             (jnp.sum(onward * state_in, axis=(1, 2)), onward)
         )
@@ -356,7 +389,7 @@
             layer_seg_block,
             layer_seg_prior,
         )
-        layer_state_in = pass_states(decay_tot, local_state)
+        decays_all, layer_state_in = gather_states(decay_tot, local_state)
         layer_mixed_out = gated_output(
             layer_pieces[0],
             layer_pieces[1],
@@ -384,21 +417,12 @@
             layer_state_in,
             layer_mixed_out,
             layer_seg_ext,
+            decays_all,
         )
         results.append(result)
         kept_all.append(saved)
         if tick_index < micro_count:
             received = passed_along(result.astype(jnp.bfloat16), "section", 1)
-    weights = unpack(
-        (
-            lax.all_gather(norm_gain, ("dp", "ctx"), axis=1, tiled=True),
-            lax.all_gather(in_weight, ("dp", "ctx"), axis=1, tiled=True),
-            lax.all_gather(conv_weight, ("dp", "ctx"), axis=2, tiled=True),
-            lax.all_gather(conv_bias, ("dp", "ctx"), axis=1, tiled=True),
-            lax.all_gather(gate_gain, ("dp", "ctx"), axis=1, tiled=True),
-            lax.all_gather(out_weight, ("dp", "ctx"), axis=1, tiled=True),
-        )
-    )
     small_sums = (
         jnp.zeros(weights[0].shape, jnp.float32),
         jnp.zeros(weights[2].shape, jnp.float32),
@@ -441,41 +465,48 @@
     proj_rows = jnp.concatenate([part_item[1] for part_item in row_parts], axis=0)
     mixed_rows = jnp.concatenate([part_item[2] for part_item in row_parts], axis=0)
     branch_rows = jnp.concatenate([part_item[3] for part_item in row_parts], axis=0)
+    proj_width = proj_rows.shape[1]
+    proj_rows = jnp.pad(proj_rows, ((0, 0), (0, -proj_width % 128)))
+    grad_outmat = lax.dot_general(
+        mixed_rows, branch_rows, (((0,), (0,)), ((), ())), preferred_element_type=jnp.float32
+    ).astype(jnp.bfloat16)
     grad_inmat = lax.dot_general(
         normed_rows, proj_rows, (((0,), (0,)), ((), ())), preferred_element_type=jnp.float32
-    )
-    grad_outmat = lax.dot_general(
-        mixed_rows, branch_rows, (((0,), (0,)), ((), ())), preferred_element_type=jnp.float32
-    )
-    taps_turned = jnp.transpose(small_sums[1])
-    owned = (
-        lax.psum_scatter(small_sums[0][None], ("dp", "ctx"), scatter_dimension=1, tiled=True),
-        lax.psum_scatter(grad_inmat[None], ("dp", "ctx"), scatter_dimension=1, tiled=True),
-        lax.psum_scatter(taps_turned[None], ("dp", "ctx"), scatter_dimension=1, tiled=True),
-        lax.psum_scatter(small_sums[2][None], ("dp", "ctx"), scatter_dimension=1, tiled=True),
-        lax.psum_scatter(small_sums[3][None], ("dp", "ctx"), scatter_dimension=1, tiled=True),
-        lax.psum_scatter(grad_outmat[None], ("dp", "ctx"), scatter_dimension=1, tiled=True),
-    )
-    head_totals = lax.psum(
-        (head_sums[0][None], head_sums[1][None], head_sums[2][None]), ("dp", "ctx")
-    )
+    ).astype(jnp.bfloat16)
+    own_outmat = lax.psum_scatter(grad_outmat, both, scatter_dimension=0, tiled=True)
+    own_inmat = lax.psum_scatter(grad_inmat, both, scatter_dimension=0, tiled=True)
+    taps_turned = small_sums[1].reshape(taps_count, shards, conv_len)
+    sums_len = small_len + 3 * a_logs.shape[0]
+    sums_width = -(-sums_len // 1024) * 1024
+    heads_row = jnp.concatenate(head_sums)
+    sums_rows = pack_small(
+        [
+            small_sums[0].reshape(shards, gain_len),
+            small_sums[3].reshape(shards, gate_len),
+            small_sums[2].reshape(shards, conv_len),
+            jnp.transpose(taps_turned, (1, 0, 2)).reshape(shards, -1),
+            jnp.broadcast_to(heads_row[None], (shards, heads_row.shape[0])),
+        ],
+        sums_width,
+    ).reshape(shards * (sums_width // 128), 128)
+    own_sums = lax.psum_scatter(sums_rows, both, scatter_dimension=0, tiled=True).reshape(-1)
+    head_totals = own_sums[small_len:sums_len].reshape(3, 1, -1)
     ends_rows = [
         jnp.where(section_index == 0, grad_inputs[micro_index + 1], results[micro_index + 1])
         for micro_index in range(micro_count)
     ]
     section_ends = jnp.stack(ends_rows)[None, :, None]
-    conv_owned = jnp.transpose(owned[2], (0, 2, 1))
     return (
         section_ends,
-        owned[0],
-        owned[1],
-        conv_owned,
-        owned[3],
+        own_sums[None, : marks[0]],
+        own_inmat[None, :, :proj_width].astype(jnp.float32),
+        own_sums[marks[2] : marks[3]].reshape(1, taps_count, conv_len),
+        own_sums[None, marks[1] : marks[2]],
         head_totals[0],
         head_totals[1],
         head_totals[2],
-        owned[4],
-        owned[5],
+        own_sums[None, marks[0] : marks[1]],
+        own_outmat[None].astype(jnp.float32),
     )
 
 

time: 1890 us -> 999 us (0.53)
  waiting for transfers between devices: 778 us -> 428 us
  starting transfers between devices: 342 us -> 20.1 us
  blocking collectives: 130 us -> 23.4 us
  local copies, waits for them, and re-layouts: 183 us -> 95.9 us
  other arithmetic: 247 us -> 221 us
    ppermute x52 -> x10, starting transfers between devices: 342 us -> 18.5 us  [passed_along(): return lax.ppermute(block, axis, route)]
    unnamed x13 -> x12, waiting for transfers between devices: 405 us -> 84.8 us
    ppermute x52 -> x10, waiting for transfers between devices: 266 us -> 25 us  [passed_along(): return lax.ppermute(block, axis, route)]
    all_gather x2 -> x8, waiting for transfers between devices: 0.04 us -> 206 us  [the longest x3 72.4 us: gather_states(): every = lax.all_gather(rows, 'ctx', axis=0, tiled=False)]
    convert_element_type x43 -> x11, other arithmetic: 54.7 us -> 4.71 us  [the longest x1 2.13 us: body(): own_inmat[None, :, :proj_width].astype(jnp.float32)]
    slice x1, local copies, waits for them, and re-layouts: 47.9 us -> 0.18 us  [conv_part(): summed = conv_offset + conv_taps[0] * extended[taps_count - 1:]]
    psum x1 -> x0, blocking collectives: 38.5 us -> none  [body(): lax.psum((head_sums[0][None], head_sums[1][None], head_sums[2][None]), ('...]
    unnamed x1 -> x0, blocking collectives: 36.6 us -> none
  transfers between devices with their start and end apart: 60 -> 21, of which waited for: 49 -> 13; matrix products, arithmetic and copies ran while one was open for 16% -> 27% of each run, Pallas kernels for 0% -> 0%
where the time goes in v1:
time: 999 us; the launch traced here: 987 us
  waiting for transfers between devices  428 us (43%)
  other arithmetic  221 us (22%)
  matrix products  171 us (17%)
  local copies, waits for them, and re-layouts  95.9 us (10%)
  between operations  26.7 us (3%)
  blocking collectives  23.4 us (2%)
  starting transfers between devices  20.1 us (2%)
    reduce_scatter x1, waiting for transfers between devices, body(): lax.psum_scatter(grad_inmat, both, scatter_dimension=0, tiled=True)  112 us
    unnamed x12, waiting for transfers between devices  84.8 us
    all_gather x3, waiting for transfers between devices, gather_states(): every = lax.all_gather(rows, 'ctx', axis=0, tiled=False)  72.4 us
    dot_general x12, matrix products, block_output(): mixed_vals = jnp.einsum('hts,shp->thp', weights, inner_vals, precision=HIGH)  58 us
    all_gather x1, waiting for transfers between devices, body(): lax.all_gather(in_weight, both, axis=1, tiled=True)[0]  49.4 us
    all_gather x1, waiting for transfers between devices, body(): lax.all_gather(out_weight, both, axis=1, tiled=True)[0]  41.9 us
    all_gather x3, waiting for transfers between devices, gather_grads(): every = lax.all_gather(rows, 'ctx', axis=0, tiled=False)  41.8 us
    ppermute x10, waiting for transfers between devices, passed_along(): return lax.ppermute(block, axis, route)  25 us
  transfers between devices with their start and end apart: 21, of which 13 were waited for; matrix products, arithmetic and copies ran while one was open for 27% of the time, Pallas kernels for 0%

profile of v1, /device:TPU:0, one launch (start us, length us, event | category | flops | bytes accessed | tf_op | source)
XLA Modules:
  0.0 986.9 jit_solution(3471323565241871917)
XLA Ops:
  10.2 23.4 %all_gather.45 = bf16[128,128]{1,0:T(8,128)(2,1)S(1)} all-gather(bf16[8,128]{1,0:T(8,128)(2,1)S(1)} %fusion.387), channel_id=1, replica_groups=mesh['section'=2,'dp'=2,'ctx'=8] {'dp','ctx'}, dimensions={0}, use_global_device_ids=true | all-gather | bytes 34816 | tf_op jit(solution)/shard_map/all_gather | solution.py:200
  43.6 49.4 %all-gather.15.cloned.1.call-done = bf16[1,1024,4384]{2,1,0:T(8,128)(2,1)} async-done(((bf16[1,64,4384]{2,1,0:T(8,128)(2,1)}), bf16[1,1024,4384]{2,1,0:T(8,128)(2,1)}) %all-gather.15.cloned.1.call-update) | async-done | bytes 8978448 | tf_op jit(solution)/shard_map/all_gather | solution.py:208
  93.0 7.3 conditional.8
  93.1 7.3 fusion.481
  110.8 2.9 divide_multiply_fusion.2
  119.0 5.2 fusion.67
  124.2 38.3 %all-gather.19.cloned.1.call-done = bf16[16512,128]{1,0:T(8,128)(2,1)} async-done(((bf16[2064,128]{1,0:T(8,128)(2,1)}), bf16[16512,128]{1,0:T(8,128)(2,1)}) %all-gather.19.cloned.1.call-update) | async-done | bytes 4227088 | tf_op jit(solution)/shard_map/all_gather | solution.py:145
  163.6 4.5 multiply_reduce_fusion.2
  172.1 41.9 %all-gather.17.cloned.1.call-done = bf16[1,2048,1024]{2,1,0:T(8,128)(2,1)} async-done(((bf16[1,128,1024]{2,1,0:T(8,128)(2,1)}), bf16[1,2048,1024]{2,1,0:T(8,128)(2,1)}) %all-gather.17.cloned.1.call-update) | async-done | bytes 4194320 | tf_op jit(solution)/shard_map/all_gather | solution.py:212
  214.0 3.7 conditional.9
  214.0 3.7 fusion.482
  221.5 4.9 collective-permute-done.1
  227.9 8.4 fusion.479
  247.8 2.9 divide_multiply_fusion.1
  261.2 5.9 fusion.76
  267.1 34.1 %all-gather.21.cloned.1.call-done = bf16[16512,128]{1,0:T(8,128)(2,1)} async-done(((bf16[2064,128]{1,0:T(8,128)(2,1)}), bf16[16512,128]{1,0:T(8,128)(2,1)}) %all-gather.21.cloned.1.call-update) | async-done | bytes 4227088 | tf_op jit(solution)/shard_map/all_gather | solution.py:145
  302.9 4.6 multiply_reduce_fusion.1
  314.1 4.6 collective-permute-start.5
  321.5 2.7 collective-permute-done.5
  330.6 6.7 broadcast_select_fusion
  352.0 5.8 select_convert_fusion
  357.9 5.5 fusion.170
  365.5 4.3 fusion.118
  372.1 2.6 multiply_reduce_fusion.23
  388.0 10.7 %fusion.171 = (f32[128,2304]{0,1:T(8,128)}, f32[128,2304]{0,1:T(8,128)}, f32[128,2304]{0,1:T(8,128)S(1)}) fusion(f32[131,2304]{0,1:T(8,128)} %get-tuple-element.395, pred[128]{0:T(512)(128)(4,1)S(1)} %get-tuple-element.491, f32[2304]{0:T(1024)S(1)} %copy-done.101, pred[128]{0:T(512)(128)(4,1)S(1)} %get-tuple-element.492, f32[2304]{0:T(1024)S(1)} %copy-done.96, ...), kind=kLoop, calls=%fused_computation.213 | loop fusion | flops 8847360 | bytes 13022976 | tf_op jit(solution)/shard_map/jvp(jit(silu))/mul | solution.py:42
  400.8 5.4 fusion.137
  406.2 25.9 %all-gather.23.cloned.1.call-done = bf16[16384,128]{1,0:T(8,128)(2,1)} async-done(((bf16[2048,128]{1,0:T(8,128)(2,1)}), bf16[16384,128]{1,0:T(8,128)(2,1)}) %all-gather.23.cloned.1.call-update) | async-done | bytes 4194320 | tf_op jit(solution)/shard_map/all_gather | solution.py:156
  432.1 4.5 fusion.2
  437.5 3.2 multiply_reduce_fusion.41
  466.0 2.5 fusion.121
  468.6 3.1 multiply_reduce_fusion.20
  481.1 3.3 fusion.183
  500.0 9.4 collective-permute-done.4
  512.9 5.0 multiply_reduce_fusion
  519.1 4.3 fusion.124
  543.9 7.0 fusion.139
  559.2 5.3 fusion.130
  564.5 16.0 %all-gather.27.cloned.1.call-done = bf16[16384,128]{1,0:T(8,128)(2,1)} async-done(((bf16[2048,128]{1,0:T(8,128)(2,1)}), bf16[16384,128]{1,0:T(8,128)(2,1)}) %all-gather.27.cloned.1.call-update) | async-done | bytes 4194320 | tf_op jit(solution)/shard_map/all_gather | solution.py:156
  580.5 4.7 fusion.1
  586.1 3.2 multiply_reduce_fusion.35
  593.9 2.8 convolution_add_fusion.3
  596.9 2.4 fusion.127
  599.4 3.1 multiply_reduce_fusion.16
  617.9 2.7 fusion.148
  620.7 7.6 fusion.289
  633.5 8.0 collective-permute-done.8
  642.3 3.2 conditional.13
  642.3 3.2 fusion.486
  645.5 2.5 multiply_reduce_fusion.24
  648.1 3.2 multiply_reduce_fusion.21
  666.0 6.5 fusion.91
  673.5 2.6 fusion.99
  676.2 2.6 multiply_reduce_fusion.27
  682.6 6.7 fusion.141
  694.5 3.3 broadcast_select_fusion.4
  699.1 5.4 convolution_convert_fusion.1
  706.2 4.5 fusion
  712.6 3.8 multiply_reduce_fusion.30
  727.1 2.6 multiply_reduce_fusion.12
  744.0 6.9 conditional.14
  744.1 6.8 fusion.487
  760.8 11.2 %convolution_convert_fusion = bf16[1024,4480]{1,0:T(8,128)(2,1)} fusion(bf16[128,4384]{0,1:T(8,128)(2,1)S(1)} %fusion.24, bf16[128,4384]{0,1:T(8,128)(2,1)} %fusion.23, bf16[128,32]{0,1:T(8,128)(2,1)} %copy-done.261, bf16[128,2304]{0,1:T(8,128)(2,1)S(1)} %copy-done.108, bf16[128,2048]{0,1:T(8,128)(2,1)S(1)} %copy-done.111, ...), kind=kOutput, calls=%fused_computation | convolution fusion | flops 3557687296 | bytes 13328384 | tf_op jit(solution)/shard_map/dot_general | solution.py:473
  779.4 83.3 %all-reduce.55.cloned.1.call-done = f32[128,128]{1,0:T(8,128)} async-done(((f32[128,128]{1,0:T(8,128)}), f32[128,128]{1,0:T(8,128)}) %all-reduce.55.cloned.1.call-update) | async-done | bytes 65552
  866.5 111.6 %reduce-scatter.3.cloned.1.call-done = bf16[64,4480]{1,0:T(8,128)(2,1)} async-done(((bf16[1024,4480]{1,0:T(8,128)(2,1)}), bf16[64,4480]{1,0:T(8,128)(2,1)}) %reduce-scatter.3.cloned.1.call-update) | async-done | bytes 573456 | tf_op jit(solution)/shard_map/reduce_scatter | solution.py:477
  (1048 shorter events, 293.0 us)
Async XLA Ops:
  7.2 31.4 %copy-start.32 = (bf16[2,1,128,1024]{3,2,1,0:T(8,128)(2,1)S(1)}, bf16[2,1,128,1024]{3,2,1,0:T(8,128)(2,1)}, u32[]{:S(2)}) copy-start(bf16[2,1,128,1024]{3,2,1,0:T(8,128)(2,1)} %param.29) | copy-start | bytes 1572868
  7.2 31.6 %copy-start.319 = (f32[1,32]{1,0:T(1,128)S(1)}, f32[1,32]{1,0:T(1,128)}, u32[]{:S(2)}) copy-start(f32[1,32]{1,0:T(1,128)} %param.37) | copy-start | bytes 388
  7.2 85.8 %all-gather.15.cloned.1.call-start = ((), (), s32[]{:S(2)}) async-start(), calls=%async_computation.2 | async-start | bytes 9748480 | tf_op jit(solution)/shard_map/all_gather | solution.py:208
  7.9 154.6 %all-gather.19.cloned.1.call-start = ((), (), s32[]{:S(2)}) async-start(), calls=%async_computation.6 | async-start | bytes 4755456 | tf_op jit(solution)/shard_map/all_gather | solution.py:145
  34.5 58.5 %copy-start.116 = (s32[2,1,1024]{2,0,1:T(2,128)}, s32[2,1,1024]{2,0,1:T(2,128)S(1)}, u32[]{:S(2)}) copy-start(s32[2,1,1024]{2,0,1:T(2,128)S(1)} %copy.755) | copy-start | bytes 24580
  35.0 75.8 %copy-start.85 = (f32[2304]{0:T(1024)}, f32[2304]{0:T(1024)S(1)}, u32[]{:S(2)}) copy-start(f32[2304]{0:T(1024)S(1)} %mul.1688) | copy-start | bytes 27652
  35.1 75.7 %copy-start.90 = (f32[2304]{0:T(1024)}, f32[2304]{0:T(1024)S(1)}, u32[]{:S(2)}) copy-start(f32[2304]{0:T(1024)S(1)} %mul.1697) | copy-start | bytes 27652
  35.2 75.6 %copy-start.95 = (f32[2304]{0:T(1024)}, f32[2304]{0:T(1024)S(1)}, u32[]{:S(2)}) copy-start(f32[2304]{0:T(1024)S(1)} %mul.1701) | copy-start | bytes 27652
  35.3 75.5 %copy-start.100 = (f32[2304]{0:T(1024)}, f32[2304]{0:T(1024)S(1)}, u32[]{:S(2)}) copy-start(f32[2304]{0:T(1024)S(1)} %mul.1704) | copy-start | bytes 27652
  35.3 75.4 %copy-start.118 = (f32[2304]{0:T(1024)}, f32[2304]{0:T(1024)S(1)}, u32[]{:S(2)}) copy-start(f32[2304]{0:T(1024)S(1)} %add.597) | copy-start | bytes 27652
  38.6 54.4 %copy-start.260 = (s32[128]{0:T(128)}, s32[128]{0:T(128)S(1)}, u32[]{:S(2)}) copy-start(s32[128]{0:T(128)S(1)} %get-tuple-element.344) | copy-start | bytes 1540
  38.8 54.3 %copy-start.262 = (f32[128]{0:T(128)}, f32[128]{0:T(128)S(1)}, u32[]{:S(2)}) copy-start(f32[128]{0:T(128)S(1)} %add_rsqrt_fusion.5) | copy-start | bytes 1540
  38.8 62.8 %copy-start.225 = (f32[32]{0:T(128)}, f32[32]{0:T(128)S(1)}, u32[]{:S(2)}) copy-start(f32[32]{0:T(128)S(1)} %exponential_bitcast_fusion) | copy-start | bytes 388
  40.7 52.3 %copy-start.258 = (s32[128]{0:T(128)}, s32[128]{0:T(128)S(1)}, u32[]{:S(2)}) copy-start(s32[128]{0:T(128)S(1)} %get-tuple-element.332) | copy-start | bytes 1540
  105.5 4.1 collective-permute-start
  116.6 97.4 %all-gather.17.cloned.1.call-start = ((), (), s32[]{:S(2)}) async-start(), calls=%async_computation.3 | async-start | bytes 4456448 | tf_op jit(solution)/shard_map/all_gather | solution.py:212
  117.3 183.9 %all-gather.21.cloned.1.call-start = ((), (), s32[]{:S(2)}) async-start(), calls=%async_computation.7 | async-start | bytes 4755456 | tf_op jit(solution)/shard_map/all_gather | solution.py:145
  171.7 139.5 %copy-start.26 = (f32[128,2048]{0,1:T(8,128)}, f32[128,2048]{0,1:T(8,128)S(1)}, u32[]{:S(2)}) copy-start(f32[128,2048]{0,1:T(8,128)S(1)} %get-tuple-element.354) | copy-start | bytes 3145732
  171.7 42.3 %copy-start.284 = (f32[128]{0:T(128)}, f32[128]{0:T(128)S(1)}, u32[]{:S(2)}) copy-start(f32[128]{0:T(128)S(1)} %add_rsqrt_fusion.4) | copy-start | bytes 1540
  218.8 7.5 collective-permute-start.1
  227.9 8.4 copy-start.308
  227.9 9.8 copy-start.155
  227.9 9.8 copy-start.226
  239.7 5.3 collective-permute-start.2
  250.8 10.3 %copy-start.36 = (f32[128,2048]{0,1:T(8,128)}, f32[128,2048]{0,1:T(8,128)S(1)}, u32[]{:S(2)}) copy-start(f32[128,2048]{0,1:T(8,128)S(1)} %slice.954) | copy-start | bytes 3145732
  253.7 178.3 %all-gather.23.cloned.1.call-start = ((), (), s32[]{:S(2)}) async-start(), calls=%async_computation.8 | async-start | bytes 4718592 | tf_op jit(solution)/shard_map/all_gather | solution.py:156
  253.9 13.1 %copy-start.210 = (s32[1,131]{1,0:T(1,128)}, s32[1,131]{1,0:T(1,128)S(1)}, u32[]{:S(2)}) copy-start(s32[1,131]{1,0:T(1,128)S(1)} %get-tuple-element.439) | copy-start | bytes 1576
  261.1 41.5 %copy-start.276 = (f32[1,32]{1,0:T(1,128)S(1)}, f32[1,32]{1,0:T(1,128)}, u32[]{:S(2)}) copy-start(f32[1,32]{1,0:T(1,128)} %copy-done.275) | copy-start | bytes 388
  312.4 8.2 copy-start.49
  314.1 10.1 %collective-permute-start.5 = (bf16[128,1024]{1,0:T(8,128)(2,1)}, bf16[128,1024]{1,0:T(8,128)(2,1)}, u32[]{:S(2)}, u32[]{:S(2)}) collective-permute-start(bf16[128,1024]{1,0:T(8,128)(2,1)} %get-tuple-element.520), channel_id=1, source_target_pairs={{0,16},{1,17},{2,18},{3,19},{4,20},{5,21},{6,22},{7,23},{8,24},{9,... | collective-permute-start | bytes 786440 | tf_op jit(solution)/shard_map/ppermute | solution.py:21
  321.4 49.4 %copy-start.25 = (f32[128,2048]{0,1:T(8,128)}, f32[128,2048]{0,1:T(8,128)S(1)}, u32[]{:S(2)}) copy-start(f32[128,2048]{0,1:T(8,128)S(1)} %get-tuple-element.218) | copy-start | bytes 3145732
  341.3 8.9 collective-permute-start.6
  363.3 12.2 %copy-start.15 = (f32[128,2304]{0,1:T(8,128)}, f32[128,2304]{0,1:T(8,128)S(1)}, u32[]{:S(2)}) copy-start(f32[128,2304]{0,1:T(8,128)S(1)} %get-tuple-element.414) | copy-start | bytes 3538948
  375.6 7.9 copy-start.303
  377.4 133.8 %all-gather.25.cloned.1.call-start = ((), (), s32[]{:S(2)}) async-start(), calls=%async_computation.9 | async-start | bytes 4755456 | tf_op jit(solution)/shard_map/all_gather | solution.py:145
  458.6 121.9 %all-gather.27.cloned.1.call-start = ((), (), s32[]{:S(2)}) async-start(), calls=%async_computation.10 | async-start | bytes 4718592 | tf_op jit(solution)/shard_map/all_gather | solution.py:156
  479.8 4.7 collective-permute-start.3
  495.0 14.4 %collective-permute-start.4 = (bf16[128,1024]{1,0:T(8,128)(2,1)}, bf16[128,1024]{1,0:T(8,128)(2,1)}, u32[]{:S(2)}, u32[]{:S(2)}) collective-permute-start(bf16[128,1024]{1,0:T(8,128)(2,1)} %fusion.274), channel_id=1, source_target_pairs={{16,0},{17,1},{18,2},{19,3},{20,4},{21,5},{22,6},{23,7},{24,8},{25... | collective-permute-start | bytes 786440 | tf_op jit(solution)/shard_map/ppermute | solution.py:21
  498.2 13.7 %copy-start.199 = (f32[8,32]{1,0:T(8,128)S(1)}, f32[8,32]{1,0:T(8,128)}, u32[]{:S(2)}) copy-start(f32[8,32]{1,0:T(8,128)} %copy-done.198) | copy-start | bytes 3076
  498.2 14.4 %copy-start.277 = (f32[1,32]{1,0:T(1,128)S(1)}, f32[1,32]{1,0:T(1,128)}, u32[]{:S(2)}) copy-start(f32[1,32]{1,0:T(1,128)} %copy-done.275) | copy-start | bytes 388
  499.3 13.4 %copy-start.114 = (f32[128,32]{0,1:T(8,128)}, f32[128,32]{0,1:T(8,128)S(1)}, u32[]{:S(2)}) copy-start(f32[128,32]{0,1:T(8,128)S(1)} %copy.653) | copy-start | bytes 49156
  499.4 19.7 %copy-start.139 = (f32[32,128]{1,0:T(8,128)}, f32[32,128]{1,0:T(8,128)S(1)}, u32[]{:S(2)}) copy-start(f32[32,128]{1,0:T(8,128)S(1)} %copy.651) | copy-start | bytes 49156
  500.0 28.7 %copy-start.147 = (f32[128,32]{0,1:T(8,128)}, f32[128,32]{0,1:T(8,128)S(1)}, u32[]{:S(2)}) copy-start(f32[128,32]{0,1:T(8,128)S(1)} %exponential_select_fusion.4) | copy-start | bytes 49156
  531.5 174.7 %all-gather.29.cloned.1.call-start = ((), (), s32[]{:S(2)}) async-start(), calls=%async_computation.11 | async-start | bytes 4718592 | tf_op jit(solution)/shard_map/all_gather | solution.py:156
  543.9 8.7 copy-start.61
  559.2 21.3 %copy-start.134 = (f32[8,2048]{1,0:T(8,128)S(1)}, f32[8,2048]{1,0:T(8,128)}, u32[]{:S(2)}) copy-start(f32[8,2048]{1,0:T(8,128)} %mul.1923) | copy-start | bytes 196612
  610.9 5.6 collective-permute-start.7
  620.7 11.1 %copy-start.66 = (f32[128,32,64]{0,2,1:T(8,128)S(1)}, f32[128,32,64]{0,2,1:T(8,128)}, u32[]{:S(2)}) copy-start(f32[128,32,64]{0,2,1:T(8,128)} %fusion.130) | copy-start | bytes 3145732
  628.4 13.9 %copy-start.2 = (bf16[1,2048,1024]{2,1,0:T(8,128)(2,1)S(1)}, bf16[1,2048,1024]{2,1,0:T(8,128)(2,1)}, u32[]{:S(2)}) copy-start(bf16[1,2048,1024]{2,1,0:T(8,128)(2,1)} %all-gather.17.cloned.1.call-done) | copy-start | bytes 12582916
  630.5 10.9 %collective-permute-start.8 = (bf16[128,1024]{1,0:T(8,128)(2,1)S(1)}, bf16[128,1024]{1,0:T(8,128)(2,1)S(1)}, u32[]{:S(2)}, u32[]{:S(2)}) collective-permute-start(bf16[128,1024]{1,0:T(8,128)(2,1)S(1)} %get-tuple-element.388), channel_id=1, source_target_pairs={{16,0},{17,1},{18,2},{19,3},{20,4},{21,5},{22,6},{23,7},{24,8},{25... | collective-permute-start | bytes 786440 | tf_op jit(solution)/shard_map/ppermute | solution.py:21
  633.4 12.0 %copy-start.28 = (f32[128,2048]{0,1:T(8,128)}, f32[128,2048]{0,1:T(8,128)S(1)}, u32[]{:S(2)}) copy-start(f32[128,2048]{0,1:T(8,128)S(1)} %get-tuple-element.299) | copy-start | bytes 3145732
  633.5 14.6 %copy-start.287 = (f32[128]{0:T(128)}, f32[128]{0:T(128)S(1)}, u32[]{:S(2)}) copy-start(f32[128]{0:T(128)S(1)} %fusion.430) | copy-start | bytes 1540
  654.1 121.4 %reduce-scatter.5.cloned.1.call-start = ((), (), s32[]{:S(2)}) async-start(), calls=%async_computation.5 | async-start | bytes 4456448 | tf_op jit(solution)/shard_map/reduce_scatter | solution.py:476
  682.6 8.4 copy-start.62
  682.6 11.9 %copy-start.68 = (f32[128,2048]{0,1:T(8,128)S(1)}, f32[128,2048]{0,1:T(8,128)}, u32[]{:S(2)}) copy-start(f32[128,2048]{0,1:T(8,128)} %get-tuple-element.330) | copy-start | bytes 3145732
  704.6 158.2 %all-reduce.55.cloned.1.call-start = ((), (), s32[]{:S(2)}) async-start(), calls=%async_computation.12 | async-start | bytes 131072
  712.6 9.8 copy-start.12
  736.5 3.9 collective-permute-start.9
  744.0 8.3 copy-start.229
  744.0 16.7 %copy-start.129 = (bf16[128,1024]{1,0:T(8,128)(2,1)S(1)}, bf16[128,1024]{1,0:T(8,128)(2,1)}, u32[]{:S(2)}) copy-start(bf16[128,1024]{1,0:T(8,128)(2,1)} %get-tuple-element.411) | copy-start | bytes 786436
  744.0 16.7 %copy-start.130 = (bf16[128,1024]{1,0:T(8,128)(2,1)S(1)}, bf16[128,1024]{1,0:T(8,128)(2,1)}, u32[]{:S(2)}) copy-start(bf16[128,1024]{1,0:T(8,128)(2,1)} %get-tuple-element.412) | copy-start | bytes 786436
  750.9 9.9 %copy-start.108 = (bf16[128,2304]{0,1:T(8,128)(2,1)S(1)}, bf16[128,2304]{0,1:T(8,128)(2,1)}, u32[]{:S(2)}) copy-start(bf16[128,2304]{0,1:T(8,128)(2,1)} %copy-done.107) | copy-start | bytes 1769476
  750.9 9.9 %copy-start.111 = (bf16[128,2048]{0,1:T(8,128)(2,1)S(1)}, bf16[128,2048]{0,1:T(8,128)(2,1)}, u32[]{:S(2)}) copy-start(bf16[128,2048]{0,1:T(8,128)(2,1)} %get-tuple-element.365) | copy-start | bytes 1572868
  760.7 217.3 %reduce-scatter.3.cloned.1.call-start = ((), (), s32[]{:S(2)}) async-start(), calls=%async_computation.4 | async-start | bytes 9748480 | tf_op jit(solution)/shard_map/reduce_scatter | solution.py:477
  (279 other events, 919.7 us)
Sparse Core Ops, SparseCore 0:
  10.4 82.6 all-gather.14
  116.7 45.7 all-gather.18
  164.7 49.2 all-gather.16
  253.9 47.2 all-gather.20
  377.5 54.5 all-gather.22
  458.7 46.6 all-gather.24
  531.7 48.7 all-gather.26
  654.2 45.2 all-gather.28
  704.7 70.7 reduce-scatter.4
  779.2 83.4 all-reduce.54
  866.9 111.1 reduce-scatter.2
